TPU v7x, 32 devices: a whole 2x2x4 slice. The times are simulated.
32 devices in a mesh: parts: 2 (over y), tile: 4 (over z), tm: 2 (over x), orb: 2 (over core).
Axes of the slice: x: 2, y: 2, z: 4, core: 2. Of those that a mesh axis runs over, the one named last changes fastest.
Arguments:
- occ_orbitals: bfloat16 [16384, 512], P('tile', ('parts', 'orb')), parts along dimension 1, may hold values from -4 to 4
- occ_tangents: bfloat16 [3, 16384, 512], P(None, 'tile', ('parts', 'orb')), parts along dimension 2, may hold values from -4 to 4
- vir_orbitals: bfloat16 [16384, 4096], P('tile', ('parts', 'orb')), parts along dimension 1, may hold values from -2 to 2
- vir_tangents: bfloat16 [3, 16384, 4096], P(None, 'tile', ('parts', 'orb')), parts along dimension 2, may hold values from -2 to 2
- occ_energy: float32 [512], P(('parts', 'orb')), parts along dimension 0, may hold values from -1 to -0.1
- occ_shift: float32 [3, 512], P(None, ('parts', 'orb')), parts along dimension 1, may hold values from -0.5 to 0.5
- vir_energy: float32 [4096], P(('parts', 'orb')), parts along dimension 0, may hold values from 0.1 to 1.5
- vir_shift: float32 [3, 4096], P(None, ('parts', 'orb')), parts along dimension 1, may hold values from -0.5 to 0.5
- time_index: int32 [2], replicated, may hold values from 0 to 11
- freq_index: int32 [2], replicated, may hold values from 0 to 11
Outputs:
- chi_tangent: bfloat16 [3, 2, 32, 16384], P(None, None, ('parts', 'orb'), ('tile', 'tm')), parts along dimension 2
There are 2 independent parts, one for each index of `parts`. A program takes and returns all parts, laid end to end along the dimension named above; an argument that names none is the same for every part. Nothing has to cross between parts.
All inputs are finite; a program needn't handle non-finite values.
Results may differ from a plain program's by a relative error of at most 0.014.
Values may be sent and summed in bfloat16 or wider, within the bound.
A program may use at most 128 MiB of HBM per device.

v0:
```python
import jax
import jax.numpy as jnp
from jax import lax
from jax.sharding import PartitionSpec as P

SLAB_DEV = 4


def time_grid(time_index, freq_index):
    tau_all = 0.1 * jnp.power(jnp.float32(1.35), time_index.astype(jnp.float32))
    omega_all = 0.2 * jnp.power(jnp.float32(1.4), freq_index.astype(jnp.float32))
    return (tau_all, 0.6 * tau_all[None, :] * jnp.cos(omega_all[:, None] * tau_all[None, :]))


def prepare_side(orbitals, tangents, weight, weight_tangent):
    scaled = (orbitals.astype(jnp.float32) * weight[None, :]).astype(jnp.bfloat16)
    moved = (
        tangents.astype(jnp.float32) * weight[None, None, :]
        + orbitals.astype(jnp.float32)[None] * weight_tangent[:, None, :]
    ).astype(jnp.bfloat16)
    return (scaled, moved)


def green_side(slab_left, slab_tangent, scaled, moved):
    green = jnp.einsum("ro,qo->rq", slab_left, scaled, preferred_element_type=jnp.float32)
    change = jnp.einsum("rmo,qo->mrq", slab_tangent, scaled, preferred_element_type=jnp.float32)
    change = change + jnp.einsum(
        "ro,mqo->mrq", slab_left, moved, preferred_element_type=jnp.float32
    )
    return (green, change)


def shards(
    occ_orbitals,
    occ_tangents,
    vir_orbitals,
    vir_tangents,
    occ_energy,
    occ_shift,
    vir_energy,
    vir_shift,
    time_index,
    freq_index,
):
    n_modes = occ_tangents.shape[0]
    n_occ = occ_orbitals.shape[1]
    n_vir = vir_orbitals.shape[1]
    n_time = time_index.shape[0]
    tau_all, weights = time_grid(time_index, freq_index)
    picked = lax.iota(jnp.int32, n_time) == lax.axis_index("tm")
    tau_now = jnp.sum(jnp.where(picked, tau_all, 0.0))
    my_column = jnp.sum(jnp.where(picked[None, :], weights, 0.0), axis=1)
    occ_weight = jnp.exp(occ_energy * tau_now)
    vir_weight = jnp.exp(-vir_energy * tau_now)
    occ_scaled, occ_moved = prepare_side(
        occ_orbitals, occ_tangents, occ_weight, tau_now * occ_shift * occ_weight[None, :]
    )
    vir_scaled, vir_moved = prepare_side(
        vir_orbitals, vir_tangents, vir_weight, -tau_now * vir_shift * vir_weight[None, :]
    )
    local_slab = jnp.concatenate(
        [
            occ_orbitals[:SLAB_DEV],
            occ_tangents[:, :SLAB_DEV].transpose(1, 0, 2).reshape(SLAB_DEV, n_modes * n_occ),
            vir_orbitals[:SLAB_DEV],
            vir_tangents[:, :SLAB_DEV].transpose(1, 0, 2).reshape(SLAB_DEV, n_modes * n_vir),
        ],
        axis=1,
    )
    occ_end = (1 + n_modes) * n_occ
    rows_piece = lax.all_gather(local_slab, "tile", axis=0, tiled=True)
    count = rows_piece.shape[0]
    occ_left = rows_piece[:, :n_occ]
    occ_left_t = rows_piece[:, n_occ:occ_end].reshape(count, n_modes, n_occ)
    vir_left = rows_piece[:, occ_end : occ_end + n_vir]
    vir_left_t = rows_piece[:, occ_end + n_vir :].reshape(count, n_modes, n_vir)
    green_occ, dgreen_occ = green_side(occ_left, occ_left_t, occ_scaled, occ_moved)
    green_vir, dgreen_vir = green_side(vir_left, vir_left_t, vir_scaled, vir_moved)
    partial_value = jnp.concatenate(
        [green_occ[None], green_vir[None], dgreen_occ, dgreen_vir], axis=0
    )
    batch_totals = lax.psum_scatter(
        partial_value.astype(jnp.bfloat16), "orb", scatter_dimension=1, tiled=True
    ).astype(jnp.float32)
    green_occ = batch_totals[0]
    green_vir = batch_totals[1]
    dgreen_occ = batch_totals[2 : 2 + n_modes]
    dgreen_vir = batch_totals[2 + n_modes :]
    chi_tau = (dgreen_occ * green_vir[None] + green_occ[None] * dgreen_vir).astype(jnp.bfloat16)
    freq_terms = my_column[None, :, None, None] * chi_tau.astype(jnp.float32)[:, None]
    result = lax.psum_scatter(
        freq_terms.astype(jnp.bfloat16), "tm", scatter_dimension=3, tiled=True
    )
    return result


def solution(mesh):
    in_specs = (
        P("tile", ("parts", "orb")),
        P(None, "tile", ("parts", "orb")),
        P("tile", ("parts", "orb")),
        P(None, "tile", ("parts", "orb")),
        P(("parts", "orb")),
        P(None, ("parts", "orb")),
        P(("parts", "orb")),
        P(None, ("parts", "orb")),
        P(),
        P(),
    )
    out_specs = P(None, None, ("parts", "orb"), ("tile", "tm"))
    return jax.shard_map(shards, mesh=mesh, in_specs=in_specs, out_specs=out_specs, check_vma=False)
```

profile of v0, /device:TPU:0, one launch (start us, length us, event | category | flops | bytes accessed | tf_op | source)
XLA Modules:
  0.0 102.5 jit_solution(4006933354464074899)
XLA Ops:
  6.5 0.0 reduce-scatter.7.cloned.1.call-start
  6.5 0.0 copy-start
  6.5 0.0 copy-start.4
  6.5 0.0 copy-start.5
  6.5 0.0 copy-start.2
  6.5 0.0 slice-start
  6.6 0.0 slice-start.1
  6.6 11.4 %convert_element_type.49 = f32[4096,1024]{1,0:T(8,128)} convert(bf16[4096,1024]{1,0:T(8,128)(2,1)} %param.12) | non-fusion elementwise | flops 4194304 | bytes 25165824 | tf_op jit(solution)/shard_map/convert_element_type | solution.py:16
  17.9 0.0 copy-done
  17.9 0.1 convert_element_type.47
  18.1 0.0 copy-done.4
  18.1 0.0 copy-done.5
  18.1 0.6 fusion.31
  19.4 0.0 copy-done.2
  19.4 0.7 multiply_exponential_fusion
  20.0 0.8 slice.39
  20.8 0.7 slice_bitcast_fusion.3
  21.5 0.0 slice-done
  21.5 0.0 slice-done.1
  21.6 15.2 %all-gather = bf16[4,4,4608]{2,1,0:T(4,128)(2,1)S(1)} all-gather(bf16[1,4,4608]{2,1,0:T(4,128)(2,1)S(1)} %maximum_bitcast_fusion), channel_id=1, replica_groups=mesh['parts'=2,'tile'=4,'tm'=2,'orb'=2] {'tile'}, dimensions={0}, use_global_device_ids=true | all-gather | bytes 184320 | tf_op jit(solution)/shard_map/all_gather | solution.py:71
  36.8 5.7 %fusion.12 = bf16[1,16,4096]{2,1,0:T(8,128)(2,1)S(1)} fusion(f32[1024]{0:T(1024)S(1)} %multiply_exponential_fusion, bf16[4096,1024]{1,0:T(8,128)(2,1)} %param.12, bf16[16,4608]{1,0:T(8,128)(2,1)S(1)} %reshape.35), kind=kOutput, calls=%fused_computation.17 | convolution fusion | flops 146866176 | bytes 8556544 | tf_op jit(solution)/shard_map/ro,qo->rq/dot_general | solution.py:25
  42.5 0.0 copy-start.7
  42.5 0.0 copy-start.3
  42.5 0.0 copy-start.6
  42.5 6.2 %fusion.3 = f32[3,16,4096]{2,1,0:T(8,128)S(1)} fusion(f32[1024]{0:T(1024)S(1)} %multiply_exponential_fusion, bf16[4096,1024]{1,0:T(8,128)(2,1)} %param.12, bf16[2,3,8,1024]{3,2,1,0:T(8,128)(2,1)S(1)} %bitcast.73), kind=kOutput, calls=%fused_computation.6 | convolution fusion | flops 415236096 | bytes 9277440 | tf_op jit(solution)/shard_map/rmo,qo->mrq/dot_general | solution.py:26
  48.7 0.0 copy-done.7
  48.7 0.0 copy-start.1
  48.7 0.7 multiply_exponential_fusion.1
  49.4 0.4 fusion.11
  49.7 0.0 copy-done.3
  49.7 0.7 multiply_multiply_fusion.1
  50.4 0.0 copy-done.6
  50.4 1.0 %convolution_bitcast_fusion = f32[3,16,4096]{2,1,0:T(8,128)S(1)} fusion(bf16[3,4096,128]{2,1,0:T(8,128)(2,1)S(1)} %copy-done.6, f32[3,128]{1,0:T(4,128)S(1)} %multiply_multiply_fusion.1, f32[4096,128]{1,0:T(8,128)S(1)} %convert_element_type.47, f32[128]{0:T(128)S(1)} %multiply_exponential_fusion.1, bf16[16,4608]{1,0:T(8,128)(2,1)S(1)} %reshape.35), kind=kOutput, calls=%fused_computation.7 | convolution fusion | flops 58195968 | bytes 6035968 | tf_op jit(solution)/shard_map/ro,mqo->mrq/dot_general | solution.py:27
  51.5 0.5 fusion.10
  52.0 0.0 copy-done.1
  52.0 15.4 %fusion.9 = bf16[3,16,4096]{2,1,0:T(8,128)(2,1)S(1)} fusion(f32[3,16,4096]{2,1,0:T(8,128)S(1)} %fusion.3, bf16[3,4096,1024]{2,1,0:T(8,128)(2,1)} %param.13, f32[3,1024]{1,0:T(4,128)S(1)} %multiply_multiply_fusion, f32[4096,1024]{1,0:T(8,128)} %convert_element_type.49, f32[1024]{0:T(1024)S(1)} %multiply_exponential_fusion, bf16[16,4608]{1,0:T(8,128)(2,1)S(1)} %reshape.35), kind=kOutput, calls=%fused_computation.12 | convolution fusion | flops 465960960 | bytes 43175936 | tf_op jit(solution)/shard_map/ro,mqo->mrq/dot_general | solution.py:27
  67.4 0.1 fusion.32
  67.5 1.0 %copy.22 = bf16[2,8,8,4096]{3,1,2,0:T(8,128)(2,1)} copy(bf16[2,8,8,4096]{3,1,0,2:T(8,128)(2,1)S(1)} %fusion.32) | data formatting | bytes 2097152
  68.6 0.0 reduce-scatter.7.cloned.1.call-update
  68.6 0.0 reduce-scatter.5.cloned.1.call-start
  68.7 0.2 select_reduce_fusion
  68.9 9.8 %reduce-scatter.7.cloned.1.call-done = bf16[8,32768]{1,0:T(8,128)(2,1)} async-done(((bf16[16,32768]{1,0:T(8,128)(2,1)}), bf16[8,32768]{1,0:T(8,128)(2,1)}) %reduce-scatter.7.cloned.1.call-update) | async-done | bytes 524304
  78.7 1.3 %copy.35 = bf16[1,8,8,4096]{3,2,1,0:T(8,128)(2,1)S(1)} copy(bf16[1,8,8,4096]{3,1,2,0:T(8,128)(2,1)} %bitcast.72) | data formatting | bytes 1048576
  80.0 0.3 copy_convert_fusion
  80.3 0.1 fusion.19
  80.4 0.9 multiply_convert_fusion.4
  81.3 0.0 reduce-scatter.5.cloned.1.call-update
  81.3 14.4 %reduce-scatter.5.cloned.1.call-done = bf16[3,2,8,2048]{3,2,1,0:T(8,128)(2,1)} async-done(((bf16[3,2,8,4096]{3,2,1,0:T(8,128)(2,1)}), bf16[3,2,8,2048]{3,2,1,0:T(8,128)(2,1)}) %reduce-scatter.5.cloned.1.call-update) | async-done | bytes 196624 | tf_op jit(solution)/shard_map/reduce_scatter | solution.py:91
  (6 shorter events, 0.1 us)
Async XLA Ops:
  6.5 72.1 %reduce-scatter.7.cloned.1.call-start = ((), (), s32[]{:S(2)}) async-start(), calls=%async_computation.3 | async-start | bytes 1572864
  6.5 11.4 %copy-start = (bf16[4096,128]{1,0:T(8,128)(2,1)S(1)}, bf16[4096,128]{1,0:T(8,128)(2,1)}, u32[]{:S(2)}) copy-start(bf16[4096,128]{1,0:T(8,128)(2,1)} %param.10) | copy-start | bytes 3145732
  6.5 11.5 %copy-start.4 = (s32[2]{0:T(128)S(1)}, s32[2]{0:T(128)}, u32[]{:S(2)}) copy-start(s32[2]{0:T(128)} %param.18) | copy-start | bytes 28
  6.5 11.6 %copy-start.5 = (s32[2]{0:T(128)S(1)}, s32[2]{0:T(128)}, u32[]{:S(2)}) copy-start(s32[2]{0:T(128)} %param.19) | copy-start | bytes 28
  6.5 12.8 %copy-start.2 = (f32[1024]{0:T(1024)S(1)}, f32[1024]{0:T(1024)}, u32[]{:S(2)}) copy-start(f32[1024]{0:T(1024)} %param.16) | copy-start | bytes 12292
  6.5 15.0 %slice-start = ((bf16[4096,1024]{1,0:T(8,128)(2,1)}), bf16[4,1024]{1,0:T(4,128)(2,1)S(1)}, s32[]{:S(2)}) async-start(bf16[4096,1024]{1,0:T(8,128)(2,1)} %param.12), calls=%async_computation.4 | async-start | bytes 16384 | tf_op jit(solution)/shard_map/slice | solution.py:65
  6.6 15.0 %slice-start.1 = ((bf16[4096,128]{1,0:T(8,128)(2,1)}), bf16[4,128]{1,0:T(4,128)(2,1)S(1)}, s32[]{:S(2)}) async-start(bf16[4096,128]{1,0:T(8,128)(2,1)} %param.10), calls=%async_computation.5 | async-start | bytes 2048 | tf_op jit(solution)/shard_map/slice | solution.py:63
  42.5 6.2 %copy-start.7 = (f32[128]{0:T(128)S(1)}, f32[128]{0:T(128)}, u32[]{:S(2)}) copy-start(f32[128]{0:T(128)} %param.14) | copy-start | bytes 1540
  42.5 7.3 %copy-start.3 = (f32[3,128]{1,0:T(4,128)S(1)}, f32[3,128]{1,0:T(4,128)}, u32[]{:S(2)}) copy-start(f32[3,128]{1,0:T(4,128)} %param.15) | copy-start | bytes 4612
  42.5 7.9 %copy-start.6 = (bf16[3,4096,128]{2,1,0:T(8,128)(2,1)S(1)}, bf16[3,4096,128]{2,1,0:T(8,128)(2,1)}, u32[]{:S(2)}) copy-start(bf16[3,4096,128]{2,1,0:T(8,128)(2,1)} %param.11) | copy-start | bytes 9437188
  48.7 3.3 %copy-start.1 = (f32[3,1024]{1,0:T(4,128)S(1)}, f32[3,1024]{1,0:T(4,128)}, u32[]{:S(2)}) copy-start(f32[3,1024]{1,0:T(4,128)} %param.17) | copy-start | bytes 36868
  68.6 27.1 %reduce-scatter.5.cloned.1.call-start = ((), (), s32[]{:S(2)}) async-start(), calls=%async_computation.2 | async-start | bytes 589824 | tf_op jit(solution)/shard_map/reduce_scatter | solution.py:91
Sparse Core Ops, SparseCore 0:
  68.7 9.8 reduce-scatter.6
  81.4 14.2 reduce-scatter.4
where the time goes:
time: 103 us
  matrix products  29.2 us (28%)
  waiting for transfers between devices  24.2 us (23%)
  other arithmetic  15.7 us (15%)
  blocking collectives  15.2 us (15%)
  between operations  14.3 us (14%)
  local copies, waits for them, and re-layouts  4 us (4%)
    dot_general x2, matrix products, green_side(): jnp.einsum('ro,mqo->mrq', slab_left, moved, preferred_element_type=jnp.fl...  16.5 us
    all_gather x1, blocking collectives, shards(): rows_piece = lax.all_gather(local_slab, 'tile', axis=0, tiled=True)  15.2 us
    reduce_scatter x1, waiting for transfers between devices, shards(): lax.psum_scatter(freq_terms.astype(jnp.bfloat16), 'tm', scatter_dimension...  14.4 us
    convert_element_type x2, other arithmetic, prepare_side(): orbitals.astype(jnp.float32) * weight[None, :]  11.5 us
    unnamed x3, waiting for transfers between devices  9.81 us
    dot_general x2, matrix products, green_side(): jnp.einsum('rmo,qo->mrq', slab_tangent, scaled, preferred_element_type=jn...  6.66 us
    dot_general x2, matrix products, green_side(): jnp.einsum('ro,qo->rq', slab_left, scaled, preferred_element_type=jnp.flo...  6.05 us
    unnamed x19, local copies, waits for them, and re-layouts  2.46 us
  transfers between devices with their start and end apart: 2, of which 2 were waited for; matrix products, arithmetic and copies ran while one was open for 0% of the time, Pallas kernels for 0%

commit v1 on v0

v1 whole, which is shorter than its diff:
```python
import functools
import math

import jax
import jax.numpy as jnp
from jax import lax
from jax.experimental import pallas as pl
from jax.experimental.pallas import tpu as pltpu
from jax.sharding import PartitionSpec as P

SLAB_DEV = 4
CHUNK = 512
MESH = pl.DeviceIdType.MESH
F32 = jnp.float32
BF16 = jnp.bfloat16


def dot_nt(left, points):
    return lax.dot_general(left, points, (((1,), (1,)), ((), ())), preferred_element_type=F32)


def kernel(
    n_tile,
    chunk,
    time_ref,
    freq_ref,
    occ_hbm,
    occ_t_hbm,
    vir_hbm,
    vir_t_hbm,
    occ_e,
    occ_s,
    vir_e,
    vir_s,
    out_ref,
    x_occ,
    x_vir,
    head_occ,
    head_vir,
    pack,
    gathered,
    slab,
    left_occ,
    left_vir,
    left0_occ,
    left0_vir,
    mine,
    outgoing,
    incoming,
    load_sem,
    head_sem,
    tile_send,
    tile_recv,
    orb_send,
    orb_recv,
):
    n_modes = occ_t_hbm.shape[0]
    groups = 1 + n_modes
    n_occ = occ_hbm.shape[1]
    n_vir = vir_hbm.shape[1]
    n_time = time_ref.shape[0]
    n_freq = freq_ref.shape[0]
    points = x_vir.shape[1]
    n_chunk = points // chunk
    rows = out_ref.shape[2]
    half = n_time * groups * rows
    me = lax.axis_index("tile")
    orb = lax.axis_index("orb")
    other = 1 - orb
    first = pl.multiple_of(lax.axis_index("tm") * points, points)

    heads = [
        pltpu.make_async_copy(occ_hbm.at[pl.ds(0, 16)], head_occ.at[0], head_sem.at[0]),
        pltpu.make_async_copy(occ_t_hbm.at[:, pl.ds(0, 16)], head_occ.at[pl.ds(1, n_modes)], head_sem.at[1]),
        pltpu.make_async_copy(vir_hbm.at[pl.ds(0, 16)], head_vir.at[0], head_sem.at[2]),
        pltpu.make_async_copy(vir_t_hbm.at[:, pl.ds(0, 16)], head_vir.at[pl.ds(1, n_modes)], head_sem.at[3]),
    ]
    for copy in heads:
        copy.start()

    barrier = pltpu.get_barrier_semaphore()
    for off in range(1, n_tile):
        pl.semaphore_signal(
            barrier, inc=1, device_id={"tile": lax.rem(me + off, n_tile)}, device_id_type=MESH
        )
    pl.semaphore_signal(barrier, inc=1, device_id={"orb": other}, device_id_type=MESH)

    loads = []
    for i in range(n_chunk):
        src = pl.ds(first + i * chunk, chunk)
        dst = pl.ds(i * chunk, chunk)
        loads.append([
            pltpu.make_async_copy(vir_hbm.at[src], x_vir.at[0, dst], load_sem.at[i, 0]),
            pltpu.make_async_copy(vir_t_hbm.at[:, src], x_vir.at[pl.ds(1, n_modes), dst], load_sem.at[i, 1]),
            pltpu.make_async_copy(occ_hbm.at[src], x_occ.at[0, dst], load_sem.at[i, 2]),
            pltpu.make_async_copy(occ_t_hbm.at[:, src], x_occ.at[pl.ds(1, n_modes), dst], load_sem.at[i, 3]),
        ])
        for copy in loads[i]:
            copy.start()

    for copy in heads:
        copy.wait()
    for g in range(groups):
        at = pl.ds(g * SLAB_DEV, SLAB_DEV)
        pack[at, :n_occ] = head_occ[g].astype(F32)[:SLAB_DEV]
        pack[at, n_occ:] = head_vir[g].astype(F32)[:SLAB_DEV]
    gathered[me] = pack[...].astype(BF16)

    pl.semaphore_wait(barrier, n_tile)
    sends = []
    for off in range(1, n_tile):
        copy = pltpu.make_async_remote_copy(
            src_ref=gathered.at[me],
            dst_ref=gathered.at[me],
            send_sem=tile_send.at[off - 1],
            recv_sem=tile_recv.at[off - 1],
            device_id={"tile": lax.rem(me + off, n_tile)},
            device_id_type=MESH,
        )
        copy.start()
        sends.append(copy)

    def tau_of(j, width):
        return 0.1 * jnp.exp(jnp.full((1, width), time_ref[j].astype(F32) * math.log(1.35), F32))

    occ_w, occ_dw, vir_w, vir_dw, freq_w = [], [], [], [], []
    for j in range(n_time):
        tau = tau_of(j, n_occ)
        weight = jnp.exp(occ_e[...].reshape(1, n_occ) * tau)
        occ_w.append(weight)
        occ_dw.append(tau * occ_s[...] * weight)
        tau = tau_of(j, n_vir)
        weight = jnp.exp(-vir_e[...].reshape(1, n_vir) * tau)
        vir_w.append(weight)
        vir_dw.append(-tau * vir_s[...] * weight)
        tau = tau_of(j, 128)
        column = []
        for k in range(n_freq):
            omega = 0.2 * jnp.exp(jnp.full((1, 128), freq_ref[k].astype(F32) * math.log(1.4), F32))
            w = 0.6 * tau * jnp.cos(omega * tau)
            column.append(jnp.concatenate([w] * (chunk // 128), axis=1))
        freq_w.append(column)

    for copy in sends:
        copy.wait_recv()

    for d in range(n_tile):
        block = gathered[d].astype(F32)
        for g in range(groups):
            slab[g, pl.ds(d * SLAB_DEV, SLAB_DEV)] = block[g * SLAB_DEV : (g + 1) * SLAB_DEV]
    for h, start in enumerate((orb, other)):
        at = pl.ds(pl.multiple_of(start * rows, rows), rows)
        for cols, width, weight, change, left, left0 in (
            (pl.ds(0, n_occ), n_occ, occ_w, occ_dw, left_occ, left0_occ),
            (pl.ds(n_occ, n_vir), n_vir, vir_w, vir_dw, left_vir, left0_vir),
        ):
            base = slab[0, at, cols]
            tangent = [slab[1 + m, at, cols] for m in range(n_modes)]
            zeroth = []
            full = []
            for j in range(n_time):
                scaled = base * weight[j]
                zeroth.append(scaled)
                full.append(scaled)
                for m in range(n_modes):
                    full.append(tangent[m] * weight[j] + base * change[j][m : m + 1])
            left[pl.ds(h * half, half)] = jnp.concatenate(full, axis=0).astype(BF16)
            left0[pl.ds(h * n_time * rows, n_time * rows)] = jnp.concatenate(zeroth, axis=0).astype(BF16)

    def exchange(i):
        return pltpu.make_async_remote_copy(
            src_ref=outgoing.at[i],
            dst_ref=incoming.at[i],
            send_sem=orb_send.at[i],
            recv_sem=orb_recv.at[i],
            device_id={"orb": other},
            device_id_type=MESH,
        )

    def partial(i):
        at = pl.ds(i * chunk, chunk)
        for copy in loads[i]:
            copy.wait()
        for side, (x, left, left0) in enumerate(
            ((x_occ, left_occ, left0_occ), (x_vir, left_vir, left0_vir))
        ):
            total = dot_nt(left[...], x[0, at])
            moved = [dot_nt(left0[...], x[1 + m, at]) for m in range(n_modes)]
            for h in range(2):
                parts = []
                for j in range(n_time):
                    for g in range(groups):
                        low = h * half + (j * groups + g) * rows
                        value = total[low : low + rows]
                        if g > 0:
                            low = (h * n_time + j) * rows
                            value = value + moved[g - 1][low : low + rows]
                        parts.append(value)
                value = jnp.concatenate(parts, axis=0)
                if h == 0:
                    mine[i, side] = value
                else:
                    outgoing[i, side] = value.astype(BF16)
        copy = exchange(i)
        copy.start()
        return copy

    def finish(i):
        at = pl.ds(i * chunk, chunk)
        green = [mine[i, side] + incoming[i, side].astype(F32) for side in range(2)]

        def pick(side, j, g):
            low = (j * groups + g) * rows
            return green[side][low : low + rows]

        for m in range(n_modes):
            chi = [
                (pick(0, j, 1 + m) * pick(1, j, 0) + pick(0, j, 0) * pick(1, j, 1 + m))
                .astype(BF16)
                .astype(F32)
                for j in range(n_time)
            ]
            for k in range(n_freq):
                total = None
                for j in range(n_time):
                    term = (freq_w[j][k] * chi[j]).astype(BF16).astype(F32)
                    total = term if total is None else total + term
                out_ref[m, k, :, at] = total.astype(BF16)

    copies = []
    for i in range(n_chunk):
        copies.append(partial(i))
        if i > 0:
            copies[i - 1].wait_recv()
            finish(i - 1)
    copies[n_chunk - 1].wait_recv()
    finish(n_chunk - 1)
    for copy in sends + copies:
        copy.wait_send()


def shards(mesh, *args):
    (occ, occ_t, vir, vir_t, occ_e, occ_s, vir_e, vir_s, time_index, freq_index) = args
    n_tile, n_tm, n_orb = mesh.shape["tile"], mesh.shape["tm"], mesh.shape["orb"]
    n_modes = occ_t.shape[0]
    groups = 1 + n_modes
    n_occ, n_vir = occ.shape[1], vir.shape[1]
    n_time, n_freq = time_index.shape[0], freq_index.shape[0]
    points = occ.shape[0] // n_tm
    chunk = min(CHUNK, points)
    n_chunk = points // chunk
    slab_rows = n_tile * SLAB_DEV
    rows = slab_rows // n_orb
    left_rows = n_time * groups * slab_rows
    half = left_rows // n_orb
    hbm = pl.BlockSpec(memory_space=pltpu.HBM)
    vmem = pl.BlockSpec(memory_space=pltpu.VMEM)
    smem = pl.BlockSpec(memory_space=pltpu.SMEM)
    dma = pltpu.SemaphoreType.DMA
    return pl.pallas_call(
        functools.partial(kernel, n_tile, chunk),
        out_shape=jax.ShapeDtypeStruct((n_modes, n_freq, rows, points), BF16),
        in_specs=[smem] * 2 + [hbm] * 4 + [vmem] * 4,
        out_specs=vmem,
        scratch_shapes=[
            pltpu.VMEM((groups, points, n_occ), BF16),
            pltpu.VMEM((groups, points, n_vir), BF16),
            pltpu.VMEM((groups, 16, n_occ), BF16),
            pltpu.VMEM((groups, 16, n_vir), BF16),
            pltpu.VMEM((groups * SLAB_DEV, n_occ + n_vir), F32),
            pltpu.VMEM((n_tile, groups * SLAB_DEV, n_occ + n_vir), BF16),
            pltpu.VMEM((groups, slab_rows, n_occ + n_vir), F32),
            pltpu.VMEM((left_rows, n_occ), BF16),
            pltpu.VMEM((left_rows, n_vir), BF16),
            pltpu.VMEM((n_time * slab_rows, n_occ), BF16),
            pltpu.VMEM((n_time * slab_rows, n_vir), BF16),
            pltpu.VMEM((n_chunk, 2, half, chunk), F32),
            pltpu.VMEM((n_chunk, 2, half, chunk), BF16),
            pltpu.VMEM((n_chunk, 2, half, chunk), BF16),
            dma((n_chunk, 4)),
            dma((4,)),
            dma((n_tile - 1,)),
            dma((n_tile - 1,)),
            dma((n_chunk,)),
            dma((n_chunk,)),
        ],
        compiler_params=pltpu.CompilerParams(
            collective_id=0, has_side_effects=True, vmem_limit_bytes=56 * 1024 * 1024
        ),
        name="polarizability_tangent",
    )(time_index, freq_index, occ, occ_t, vir, vir_t, occ_e, occ_s, vir_e, vir_s)


def solution(mesh):
    in_specs = (
        P("tile", ("parts", "orb")),
        P(None, "tile", ("parts", "orb")),
        P("tile", ("parts", "orb")),
        P(None, "tile", ("parts", "orb")),
        P(("parts", "orb")),
        P(None, ("parts", "orb")),
        P(("parts", "orb")),
        P(None, ("parts", "orb")),
        P(),
        P(),
    )
    out_specs = P(None, None, ("parts", "orb"), ("tile", "tm"))
    return jax.shard_map(
        functools.partial(shards, mesh),
        mesh=mesh,
        in_specs=in_specs,
        out_specs=out_specs,
        check_vma=False,
    )
```

time: 103 us -> 19.9 us (0.19)
  matrix products: 29.2 us -> 0 us
  waiting for transfers between devices: 24.2 us -> 0 us
  Pallas kernels: 0 us -> 18 us
  other arithmetic: 15.7 us -> 0 us
  blocking collectives: 15.2 us -> 0 us
  between operations: 14.3 us -> 0.01 us
  local copies, waits for them, and re-layouts: 4 us -> 1.62 us
    dot_general x6 -> x0, matrix products: 29.2 us -> none  [the longest x2 16.5 us: green_side(): jnp.einsum('ro,mqo->mrq', slab_left, moved, preferred_element_type=jnp.fl...]
    pallas_call x0 -> x1, Pallas kernels: none -> 18 us  [shards(): pl.pallas_call(functools.partial(kernel, n_tile, chunk), out_shape=jax.Sh...]
    all_gather x1 -> x0, blocking collectives: 15.2 us -> none  [shards(): rows_piece = lax.all_gather(local_slab, 'tile', axis=0, tiled=True)]
    reduce_scatter x1 -> x0, waiting for transfers between devices: 14.4 us -> none  [shards(): lax.psum_scatter(freq_terms.astype(jnp.bfloat16), 'tm', scatter_dimension...]
    convert_element_type x5 -> x0, other arithmetic: 12.7 us -> none  [the longest x2 11.5 us: prepare_side(): orbitals.astype(jnp.float32) * weight[None, :]]
    unnamed x3 -> x0, waiting for transfers between devices: 9.81 us -> none
    exp x2 -> x0, other arithmetic: 1.31 us -> none  [the longest x1 0.66 us: shards(): occ_weight = jnp.exp(occ_energy * tau_now)]
    mul x3 -> x0, other arithmetic: 1.29 us -> none  [the longest x1 0.67 us: shards(): tau_now * occ_shift * occ_weight[None, :]]
  transfers between devices with their start and end apart: 2 -> 0, of which waited for: 2 -> 0; matrix products, arithmetic and copies ran while one was open for 0% -> 0% of each run, Pallas kernels for 0% -> 0%
where the time goes in v1:
time: 19.9 us; the launch traced here: 19.6 us
  Pallas kernels  18 us (90%)
  local copies, waits for them, and re-layouts  1.62 us (8%)
    pallas_call x1, Pallas kernels, shards(): pl.pallas_call(functools.partial(kernel, n_tile, chunk), out_shape=jax.Sh...  18 us
    unnamed x1, local copies, waits for them, and re-layouts  1.62 us

profile of v1, /device:TPU:0, one launch (start us, length us, event | category | flops | bytes accessed | tf_op | source)
XLA Modules:
  0.0 19.6 jit_solution(5589251499935225030)
XLA Ops:
  0.0 18.0 %polarizability_tangent.1 = bf16[3,2,8,2048]{3,2,1,0:T(8,128)(2,1)} custom-call(s32[2]{0:T(128)} %time_ref.1, s32[2]{0:T(128)} %freq_ref.1, bf16[4096,128]{1,0:T(8,128)(2,1)} %occ_hbm.1, bf16[3,4096,128]{2,1,0:T(8,128)(2,1)} %occ_t_hbm.1, bf16[4096,1024]{1,0:T(8,128)(2,1)} %vir_hbm.1, bf16[3,4096,1024]{2,1,0:T(8,128)(2,1)} %vir_t_hbm.1, f32[128]{0:T(128)} %occ_e.1, ...), custom_call_target="tpu_custom_call" | custom-call | tf_op jit(solution)/shard_map/polarizability_tangent/pallas_call | solution.py:260
  18.0 1.6 %copy.12 = bf16[3,2,8,2048]{3,2,1,0:T(8,128)(2,1)} copy(bf16[3,2,8,2048]{3,2,1,0:T(8,128)(2,1)} %polarizability_tangent.1) | data formatting | bytes 393216

commit v2 on v1

--- a/solution.py
+++ b/solution.py
@@ -9,7 +9,7 @@
 from jax.sharding import PartitionSpec as P
 
 SLAB_DEV = 4
-CHUNK = 512
+CHUNKS = (512, 512, 512, 512)
 MESH = pl.DeviceIdType.MESH
 F32 = jnp.float32
 BF16 = jnp.bfloat16
@@ -21,18 +21,26 @@
 
 def kernel(
     n_tile,
-    chunk,
-    time_ref,
-    freq_ref,
+    chunks,
+    time_hbm,
+    freq_hbm,
     occ_hbm,
     occ_t_hbm,
     vir_hbm,
     vir_t_hbm,
+    occ_e_hbm,
+    occ_s_hbm,
+    vir_e_hbm,
+    vir_s_hbm,
+    out_ref,
+    time_ref,
+    freq_ref,
     occ_e,
     occ_s,
     vir_e,
     vir_s,
-    out_ref,
+    weights,
+    columns,
     x_occ,
     x_vir,
     head_occ,
@@ -42,13 +50,13 @@
     slab,
     left_occ,
     left_vir,
-    left0_occ,
     left0_vir,
     mine,
     outgoing,
     incoming,
     load_sem,
     head_sem,
+    small_sem,
     tile_send,
     tile_recv,
     orb_send,
@@ -61,7 +69,8 @@
     n_time = time_ref.shape[0]
     n_freq = freq_ref.shape[0]
     points = x_vir.shape[1]
-    n_chunk = points // chunk
+    n_chunk = len(chunks)
+    starts = [sum(chunks[:i]) for i in range(n_chunk)]
     rows = out_ref.shape[2]
     half = n_time * groups * rows
     me = lax.axis_index("tile")
@@ -85,10 +94,23 @@
         )
     pl.semaphore_signal(barrier, inc=1, device_id={"orb": other}, device_id_type=MESH)
 
+    smalls = [
+        pltpu.make_async_copy(src, dst, small_sem.at[at])
+        for at, (src, dst) in enumerate((
+            (time_hbm, time_ref),
+            (freq_hbm, freq_ref),
+            (occ_e_hbm, occ_e),
+            (occ_s_hbm, occ_s),
+            (vir_e_hbm, vir_e),
+            (vir_s_hbm, vir_s),
+        ))
+    ]
+    for copy in smalls:
+        copy.start()
     loads = []
     for i in range(n_chunk):
-        src = pl.ds(first + i * chunk, chunk)
-        dst = pl.ds(i * chunk, chunk)
+        src = pl.ds(first + starts[i], chunks[i])
+        dst = pl.ds(starts[i], chunks[i])
         loads.append([
             pltpu.make_async_copy(vir_hbm.at[src], x_vir.at[0, dst], load_sem.at[i, 0]),
             pltpu.make_async_copy(vir_t_hbm.at[:, src], x_vir.at[pl.ds(1, n_modes), dst], load_sem.at[i, 1]),
@@ -123,24 +145,26 @@
     def tau_of(j, width):
         return 0.1 * jnp.exp(jnp.full((1, width), time_ref[j].astype(F32) * math.log(1.35), F32))
 
-    occ_w, occ_dw, vir_w, vir_dw, freq_w = [], [], [], [], []
+    for copy in smalls:
+        copy.wait()
+    occ_cols, vir_cols = pl.ds(0, n_occ), pl.ds(n_occ, n_vir)
     for j in range(n_time):
-        tau = tau_of(j, n_occ)
-        weight = jnp.exp(occ_e[...].reshape(1, n_occ) * tau)
-        occ_w.append(weight)
-        occ_dw.append(tau * occ_s[...] * weight)
-        tau = tau_of(j, n_vir)
-        weight = jnp.exp(-vir_e[...].reshape(1, n_vir) * tau)
-        vir_w.append(weight)
-        vir_dw.append(-tau * vir_s[...] * weight)
+        for cols, width, energy, shift, sign in (
+            (occ_cols, n_occ, occ_e, occ_s, 1.0),
+            (vir_cols, n_vir, vir_e, vir_s, -1.0),
+        ):
+            tau = sign * tau_of(j, width)
+            weight = jnp.exp(energy[...].reshape(1, width) * tau)
+            weights[j, pl.ds(0, 1), cols] = weight
+            weights[j, pl.ds(1, n_modes), cols] = tau * shift[...] * weight
         tau = tau_of(j, 128)
-        column = []
         for k in range(n_freq):
             omega = 0.2 * jnp.exp(jnp.full((1, 128), freq_ref[k].astype(F32) * math.log(1.4), F32))
-            w = 0.6 * tau * jnp.cos(omega * tau)
-            column.append(jnp.concatenate([w] * (chunk // 128), axis=1))
-        freq_w.append(column)
-
+            columns[j, pl.ds(k, 1)] = 0.6 * tau * jnp.cos(omega * tau)
+
+    for i in range(n_chunk):
+        for copy in loads[i]:
+            copy.wait()
     for copy in sends:
         copy.wait_recv()
 
@@ -150,27 +174,32 @@
             slab[g, pl.ds(d * SLAB_DEV, SLAB_DEV)] = block[g * SLAB_DEV : (g + 1) * SLAB_DEV]
     for h, start in enumerate((orb, other)):
         at = pl.ds(pl.multiple_of(start * rows, rows), rows)
-        for cols, width, weight, change, left, left0 in (
-            (pl.ds(0, n_occ), n_occ, occ_w, occ_dw, left_occ, left0_occ),
-            (pl.ds(n_occ, n_vir), n_vir, vir_w, vir_dw, left_vir, left0_vir),
-        ):
+        for cols, width, left in ((occ_cols, n_occ, left_occ), (vir_cols, n_vir, left_vir)):
             base = slab[0, at, cols]
             tangent = [slab[1 + m, at, cols] for m in range(n_modes)]
+            zero = jnp.zeros_like(base)
             zeroth = []
             full = []
             for j in range(n_time):
-                scaled = base * weight[j]
-                zeroth.append(scaled)
-                full.append(scaled)
+                weight = weights[j, pl.ds(0, 1), cols]
+                zeroth.append(base * weight)
+                full.append(zeroth[j])
                 for m in range(n_modes):
-                    full.append(tangent[m] * weight[j] + base * change[j][m : m + 1])
-            left[pl.ds(h * half, half)] = jnp.concatenate(full, axis=0).astype(BF16)
-            left0[pl.ds(h * n_time * rows, n_time * rows)] = jnp.concatenate(zeroth, axis=0).astype(BF16)
+                    full.append(tangent[m] * weight + base * weights[j, pl.ds(1 + m, 1), cols])
+            left[pl.ds(h * half, half), pl.ds(0, width)] = jnp.concatenate(full, axis=0).astype(BF16)
+            if left is left_vir:
+                value = jnp.concatenate(zeroth, axis=0).astype(BF16)
+                left0_vir[pl.ds(h * n_time * rows, n_time * rows)] = value
+                continue
+            for g in range(1, groups):
+                full = [zeroth[j] if g == at_g else zero for j in range(n_time) for at_g in range(groups)]
+                value = jnp.concatenate(full, axis=0).astype(BF16)
+                left[pl.ds(h * half, half), pl.ds(g * width, width)] = value
 
     def exchange(i):
         return pltpu.make_async_remote_copy(
-            src_ref=outgoing.at[i],
-            dst_ref=incoming.at[i],
+            src_ref=outgoing.at[:, :, pl.ds(starts[i], chunks[i])],
+            dst_ref=incoming.at[:, :, pl.ds(starts[i], chunks[i])],
             send_sem=orb_send.at[i],
             recv_sem=orb_recv.at[i],
             device_id={"orb": other},
@@ -178,36 +207,35 @@
         )
 
     def partial(i):
-        at = pl.ds(i * chunk, chunk)
-        for copy in loads[i]:
-            copy.wait()
-        for side, (x, left, left0) in enumerate(
-            ((x_occ, left_occ, left0_occ), (x_vir, left_vir, left0_vir))
-        ):
-            total = dot_nt(left[...], x[0, at])
-            moved = [dot_nt(left0[...], x[1 + m, at]) for m in range(n_modes)]
-            for h in range(2):
-                parts = []
-                for j in range(n_time):
-                    for g in range(groups):
-                        low = h * half + (j * groups + g) * rows
-                        value = total[low : low + rows]
-                        if g > 0:
-                            low = (h * n_time + j) * rows
-                            value = value + moved[g - 1][low : low + rows]
-                        parts.append(value)
-                value = jnp.concatenate(parts, axis=0)
-                if h == 0:
-                    mine[i, side] = value
-                else:
-                    outgoing[i, side] = value.astype(BF16)
+        at = pl.ds(starts[i], chunks[i])
+        joined = jnp.concatenate([x_occ[g, at] for g in range(groups)], axis=1)
+        value = dot_nt(left_occ[...], joined)
+        mine[0, :, at] = value[:half]
+        outgoing[0, :, at] = value[half:].astype(BF16)
+        total = dot_nt(left_vir[...], x_vir[0, at])
+        moved = [dot_nt(left0_vir[...], x_vir[1 + m, at]) for m in range(n_modes)]
+        for h in range(2):
+            parts = []
+            for j in range(n_time):
+                for g in range(groups):
+                    low = h * half + (j * groups + g) * rows
+                    value = total[low : low + rows]
+                    if g > 0:
+                        low = (h * n_time + j) * rows
+                        value = value + moved[g - 1][low : low + rows]
+                    parts.append(value)
+            value = jnp.concatenate(parts, axis=0)
+            if h == 0:
+                mine[1, :, at] = value
+            else:
+                outgoing[1, :, at] = value.astype(BF16)
         copy = exchange(i)
         copy.start()
         return copy
 
     def finish(i):
-        at = pl.ds(i * chunk, chunk)
-        green = [mine[i, side] + incoming[i, side].astype(F32) for side in range(2)]
+        at = pl.ds(starts[i], chunks[i])
+        green = [mine[side, :, at] + incoming[side, :, at].astype(F32) for side in range(2)]
 
         def pick(side, j, g):
             low = (j * groups + g) * rows
@@ -223,7 +251,8 @@
             for k in range(n_freq):
                 total = None
                 for j in range(n_time):
-                    term = (freq_w[j][k] * chi[j]).astype(BF16).astype(F32)
+                    column = jnp.concatenate([columns[j, pl.ds(k, 1)]] * (chunks[i] // 128), axis=1)
+                    term = (column * chi[j]).astype(BF16).astype(F32)
                     total = term if total is None else total + term
                 out_ref[m, k, :, at] = total.astype(BF16)
 
@@ -247,22 +276,30 @@
     n_occ, n_vir = occ.shape[1], vir.shape[1]
     n_time, n_freq = time_index.shape[0], freq_index.shape[0]
     points = occ.shape[0] // n_tm
-    chunk = min(CHUNK, points)
-    n_chunk = points // chunk
+    chunks = CHUNKS if points == sum(CHUNKS) else (points,)
+    n_chunk = len(chunks)
     slab_rows = n_tile * SLAB_DEV
     rows = slab_rows // n_orb
     left_rows = n_time * groups * slab_rows
     half = left_rows // n_orb
     hbm = pl.BlockSpec(memory_space=pltpu.HBM)
     vmem = pl.BlockSpec(memory_space=pltpu.VMEM)
-    smem = pl.BlockSpec(memory_space=pltpu.SMEM)
+    smem = pltpu.SMEM
     dma = pltpu.SemaphoreType.DMA
     return pl.pallas_call(
-        functools.partial(kernel, n_tile, chunk),
+        functools.partial(kernel, n_tile, chunks),
         out_shape=jax.ShapeDtypeStruct((n_modes, n_freq, rows, points), BF16),
-        in_specs=[smem] * 2 + [hbm] * 4 + [vmem] * 4,
+        in_specs=[hbm] * 10,
         out_specs=vmem,
         scratch_shapes=[
+            smem((n_time,), jnp.int32),
+            smem((n_freq,), jnp.int32),
+            pltpu.VMEM((n_occ,), F32),
+            pltpu.VMEM((n_modes, n_occ), F32),
+            pltpu.VMEM((n_vir,), F32),
+            pltpu.VMEM((n_modes, n_vir), F32),
+            pltpu.VMEM((n_time, groups, n_occ + n_vir), F32),
+            pltpu.VMEM((n_time, n_freq, 128), F32),
             pltpu.VMEM((groups, points, n_occ), BF16),
             pltpu.VMEM((groups, points, n_vir), BF16),
             pltpu.VMEM((groups, 16, n_occ), BF16),
@@ -270,15 +307,15 @@
             pltpu.VMEM((groups * SLAB_DEV, n_occ + n_vir), F32),
             pltpu.VMEM((n_tile, groups * SLAB_DEV, n_occ + n_vir), BF16),
             pltpu.VMEM((groups, slab_rows, n_occ + n_vir), F32),
-            pltpu.VMEM((left_rows, n_occ), BF16),
+            pltpu.VMEM((left_rows, groups * n_occ), BF16),
             pltpu.VMEM((left_rows, n_vir), BF16),
-            pltpu.VMEM((n_time * slab_rows, n_occ), BF16),
             pltpu.VMEM((n_time * slab_rows, n_vir), BF16),
-            pltpu.VMEM((n_chunk, 2, half, chunk), F32),
-            pltpu.VMEM((n_chunk, 2, half, chunk), BF16),
-            pltpu.VMEM((n_chunk, 2, half, chunk), BF16),
+            pltpu.VMEM((2, half, points), F32),
+            pltpu.VMEM((2, half, points), BF16),
+            pltpu.VMEM((2, half, points), BF16),
             dma((n_chunk, 4)),
             dma((4,)),
+            dma((6,)),
             dma((n_tile - 1,)),
             dma((n_tile - 1,)),
             dma((n_chunk,)),

time: 19.9 us -> 18.9 us (0.950)
  Pallas kernels: 18 us -> 17 us
    pallas_call x1, Pallas kernels: 18 us -> 17 us  [shards(): pl.pallas_call(functools.partial(kernel, n_tile, chunks), out_shape=jax.S...]
where the time goes in v2:
time: 18.9 us; the launch traced here: 18.6 us
  Pallas kernels  17 us (90%)
  local copies, waits for them, and re-layouts  1.62 us (9%)
    pallas_call x1, Pallas kernels, shards(): pl.pallas_call(functools.partial(kernel, n_tile, chunks), out_shape=jax.S...  17 us
    unnamed x1, local copies, waits for them, and re-layouts  1.62 us

profile of v2, /device:TPU:0, one launch (start us, length us, event | category | flops | bytes accessed | tf_op | source)
XLA Modules:
  0.0 18.6 jit_solution(7192476632432699960)
XLA Ops:
  0.0 17.0 %polarizability_tangent.1 = bf16[3,2,8,2048]{3,2,1,0:T(8,128)(2,1)} custom-call(s32[2]{0:T(128)} %time_hbm.1, s32[2]{0:T(128)} %freq_hbm.1, bf16[4096,128]{1,0:T(8,128)(2,1)} %occ_hbm.1, bf16[3,4096,128]{2,1,0:T(8,128)(2,1)} %occ_t_hbm.1, bf16[4096,1024]{1,0:T(8,128)(2,1)} %vir_hbm.1, bf16[3,4096,1024]{2,1,0:T(8,128)(2,1)} %vir_t_hbm.1, f32[128]{0:T(128)} %occ_e_hbm.1, ...), custom_call_target="tpu_custom_call" | custom-call | tf_op jit(solution)/shard_map/polarizability_tangent/pallas_call | solution.py:289
  17.0 1.6 %copy.12 = bf16[3,2,8,2048]{3,2,1,0:T(8,128)(2,1)} copy(bf16[3,2,8,2048]{3,2,1,0:T(8,128)(2,1)} %polarizability_tangent.1) | data formatting | bytes 393216

commit v3 on v2

--- a/solution.py
+++ b/solution.py
@@ -9,7 +9,7 @@
 from jax.sharding import PartitionSpec as P
 
 SLAB_DEV = 4
-CHUNKS = (512, 512, 512, 512)
+CHUNKS = (2048,)
 MESH = pl.DeviceIdType.MESH
 F32 = jnp.float32
 BF16 = jnp.bfloat16
@@ -50,7 +50,6 @@
     slab,
     left_occ,
     left_vir,
-    left0_vir,
     mine,
     outgoing,
     incoming,
@@ -78,6 +77,13 @@
     other = 1 - orb
     first = pl.multiple_of(lax.axis_index("tm") * points, points)
 
+    barrier = pltpu.get_barrier_semaphore()
+    for off in range(1, n_tile):
+        pl.semaphore_signal(
+            barrier, inc=1, device_id={"tile": lax.rem(me + off, n_tile)}, device_id_type=MESH
+        )
+    pl.semaphore_signal(barrier, inc=1, device_id={"orb": other}, device_id_type=MESH)
+
     heads = [
         pltpu.make_async_copy(occ_hbm.at[pl.ds(0, 16)], head_occ.at[0], head_sem.at[0]),
         pltpu.make_async_copy(occ_t_hbm.at[:, pl.ds(0, 16)], head_occ.at[pl.ds(1, n_modes)], head_sem.at[1]),
@@ -86,13 +92,6 @@
     ]
     for copy in heads:
         copy.start()
-
-    barrier = pltpu.get_barrier_semaphore()
-    for off in range(1, n_tile):
-        pl.semaphore_signal(
-            barrier, inc=1, device_id={"tile": lax.rem(me + off, n_tile)}, device_id_type=MESH
-        )
-    pl.semaphore_signal(barrier, inc=1, device_id={"orb": other}, device_id_type=MESH)
 
     smalls = [
         pltpu.make_async_copy(src, dst, small_sem.at[at])
@@ -117,11 +116,11 @@
             pltpu.make_async_copy(occ_hbm.at[src], x_occ.at[0, dst], load_sem.at[i, 2]),
             pltpu.make_async_copy(occ_t_hbm.at[:, src], x_occ.at[pl.ds(1, n_modes), dst], load_sem.at[i, 3]),
         ])
+    for copy in heads:
+        copy.wait()
+    for i in range(n_chunk):
         for copy in loads[i]:
             copy.start()
-
-    for copy in heads:
-        copy.wait()
     for g in range(groups):
         at = pl.ds(g * SLAB_DEV, SLAB_DEV)
         pack[at, :n_occ] = head_occ[g].astype(F32)[:SLAB_DEV]
@@ -187,10 +186,6 @@
                 for m in range(n_modes):
                     full.append(tangent[m] * weight + base * weights[j, pl.ds(1 + m, 1), cols])
             left[pl.ds(h * half, half), pl.ds(0, width)] = jnp.concatenate(full, axis=0).astype(BF16)
-            if left is left_vir:
-                value = jnp.concatenate(zeroth, axis=0).astype(BF16)
-                left0_vir[pl.ds(h * n_time * rows, n_time * rows)] = value
-                continue
             for g in range(1, groups):
                 full = [zeroth[j] if g == at_g else zero for j in range(n_time) for at_g in range(groups)]
                 value = jnp.concatenate(full, axis=0).astype(BF16)
@@ -208,27 +203,11 @@
 
     def partial(i):
         at = pl.ds(starts[i], chunks[i])
-        joined = jnp.concatenate([x_occ[g, at] for g in range(groups)], axis=1)
-        value = dot_nt(left_occ[...], joined)
-        mine[0, :, at] = value[:half]
-        outgoing[0, :, at] = value[half:].astype(BF16)
-        total = dot_nt(left_vir[...], x_vir[0, at])
-        moved = [dot_nt(left0_vir[...], x_vir[1 + m, at]) for m in range(n_modes)]
-        for h in range(2):
-            parts = []
-            for j in range(n_time):
-                for g in range(groups):
-                    low = h * half + (j * groups + g) * rows
-                    value = total[low : low + rows]
-                    if g > 0:
-                        low = (h * n_time + j) * rows
-                        value = value + moved[g - 1][low : low + rows]
-                    parts.append(value)
-            value = jnp.concatenate(parts, axis=0)
-            if h == 0:
-                mine[1, :, at] = value
-            else:
-                outgoing[1, :, at] = value.astype(BF16)
+        for side, (x, left) in enumerate(((x_occ, left_occ), (x_vir, left_vir))):
+            joined = jnp.concatenate([x[g, at] for g in range(groups)], axis=1)
+            value = dot_nt(joined, left[...]).T
+            mine[side, :, at] = value[:half]
+            outgoing[side, :, at] = value[half:].astype(BF16)
         copy = exchange(i)
         copy.start()
         return copy
@@ -308,8 +287,7 @@
             pltpu.VMEM((n_tile, groups * SLAB_DEV, n_occ + n_vir), BF16),
             pltpu.VMEM((groups, slab_rows, n_occ + n_vir), F32),
             pltpu.VMEM((left_rows, groups * n_occ), BF16),
-            pltpu.VMEM((left_rows, n_vir), BF16),
-            pltpu.VMEM((n_time * slab_rows, n_vir), BF16),
+            pltpu.VMEM((left_rows, groups * n_vir), BF16),
             pltpu.VMEM((2, half, points), F32),
             pltpu.VMEM((2, half, points), BF16),
             pltpu.VMEM((2, half, points), BF16),

time: 18.9 us -> 18.3 us (0.968)
  Pallas kernels: 17 us -> 16.4 us
    pallas_call x1, Pallas kernels: 17 us -> 16.4 us  [shards(): pl.pallas_call(functools.partial(kernel, n_tile, chunks), out_shape=jax.S...]
where the time goes in v3:
time: 18.3 us; the launch traced here: 18 us
  Pallas kernels  16.4 us (90%)
  local copies, waits for them, and re-layouts  1.62 us (9%)
    pallas_call x1, Pallas kernels, shards(): pl.pallas_call(functools.partial(kernel, n_tile, chunks), out_shape=jax.S...  16.4 us
    unnamed x1, local copies, waits for them, and re-layouts  1.62 us

profile of v3, /device:TPU:0, one launch (start us, length us, event | category | flops | bytes accessed | tf_op | source)
XLA Modules:
  0.0 18.0 jit_solution(5001302253198649010)
XLA Ops:
  0.0 16.4 %polarizability_tangent.1 = bf16[3,2,8,2048]{3,2,1,0:T(8,128)(2,1)} custom-call(s32[2]{0:T(128)} %time_hbm.1, s32[2]{0:T(128)} %freq_hbm.1, bf16[4096,128]{1,0:T(8,128)(2,1)} %occ_hbm.1, bf16[3,4096,128]{2,1,0:T(8,128)(2,1)} %occ_t_hbm.1, bf16[4096,1024]{1,0:T(8,128)(2,1)} %vir_hbm.1, bf16[3,4096,1024]{2,1,0:T(8,128)(2,1)} %vir_t_hbm.1, f32[128]{0:T(128)} %occ_e_hbm.1, ...), custom_call_target="tpu_custom_call" | custom-call | tf_op jit(solution)/shard_map/polarizability_tangent/pallas_call | solution.py:268
  16.4 1.6 %copy.12 = bf16[3,2,8,2048]{3,2,1,0:T(8,128)(2,1)} copy(bf16[3,2,8,2048]{3,2,1,0:T(8,128)(2,1)} %polarizability_tangent.1) | data formatting | bytes 393216
